TPU v7x, 32 devices: a whole 2x2x4 slice. The times are simulated.
32 devices in a mesh: groups: 2 (over x), chan: 16 (over z, y, core).
Axes of the slice: x: 2, y: 2, z: 4, core: 2. Of those that a mesh axis runs over, the one named last changes fastest.
Arguments:
- voltages: int32 [4096, 79, 2048], P(('groups', 'chan')), parts along dimension 0, may hold values from -96 to 96, as said below
- input_mask: int32 [4096], P(('groups', 'chan')), parts along dimension 0, may hold values 0 or 1
- fir_taps: float32 [16, 2048], replicated, may hold values from -1.5 to 1.5
Outputs:
- visibilities: bfloat16 [32768, 2048], P(('groups', 'chan')), parts along dimension 0
There are 2 independent parts, one for each index of `groups`. A program takes and returns all parts, laid end to end along the dimension named above; an argument that names none is the same for every part. Nothing has to cross between parts.
Inputs may be any that keep to these rules, and one draw needn't show every extreme that they name: `voltages`: 8-bit voltage samples; each input's amplitude, colour and share of a common signal differ.
All inputs are finite; a program needn't handle non-finite values. No bound on the sum of `input_mask` on one device may be relied on, other than what follows from the above.
Results may differ from a plain program's by a relative error of at most 0.006.
Values may be sent and summed in bfloat16 or wider, within the bound.
A program may use at most 320 MiB of HBM per device.

v0:
```python
from functools import reduce
import math
import jax
import jax.numpy as jnp
from jax import lax
from jax.sharding import PartitionSpec as P

INPUTS = 2048
NFFT = 2048
TAPS = 16
SPEC = 64
epsilon = 1e-05


def swapped(value, axis, stride):
    return lax.ppermute(value, axis, [(i, i ^ 1 << stride) for i in range(lax.axis_size(axis))])


def dft_matrix(length, channels):
    column = jnp.arange(length, dtype=jnp.int32)[:, None]
    channel = jnp.arange(1, channels + 1, dtype=jnp.int32)[None, :]
    phases = column * channel % length
    angles = phases.astype(jnp.float32) * (2.0 * math.pi / length)
    return jnp.concatenate([jnp.cos(angles), -jnp.sin(angles)], axis=1).astype(jnp.bfloat16)


def add_terms(left, right):
    return left + right


def polyphase(voltages, input_mask, fir_taps):
    samples = (voltages * input_mask[:, None, None]).astype(jnp.bfloat16)
    terms = [
        fir_taps[offset][None, None, :] * samples[:, offset : offset + SPEC, :]
        for offset in range(TAPS)
    ]
    filtered = reduce(add_terms, terms)
    return filtered.astype(jnp.bfloat16)


def contract(left, right):
    return lax.dot_general(
        left, right, (((1,), (1,)), ((), ())), preferred_element_type=jnp.float32
    )


def on_device(voltages, input_mask, fir_taps):
    devices = lax.axis_size("chan")
    channels = devices // 2
    local_inputs = voltages.shape[0]
    filtered = polyphase(voltages, input_mask, fir_taps)
    spectra = jnp.einsum(
        "isn,nk->iks", filtered, dft_matrix(NFFT, channels), preferred_element_type=jnp.float32
    )
    squares = jnp.sum(spectra * spectra, axis=(0, 2))
    band_partial = squares[:channels] + squares[channels:]
    band_total = lax.psum(band_partial, "chan")
    channel_gain = lax.rsqrt(band_total / (INPUTS * SPEC) + epsilon)
    equalized = (spectra * jnp.concatenate([channel_gain, channel_gain])[None, :, None]).astype(
        jnp.bfloat16
    )
    by_channel = equalized.reshape(local_inputs, 2, channels, SPEC)
    parity = lax.axis_index("chan") % 2
    half_rows = INPUTS // 2
    half_spec = SPEC // 2
    outgoing = by_channel.reshape(local_inputs, 2, channels, 2, half_spec)
    outgoing = outgoing.transpose(2, 3, 0, 1, 4).reshape(devices, local_inputs, SPEC)
    received = lax.all_to_all(outgoing, "chan", split_axis=0, concat_axis=1, tiled=True)[0]
    real_part = received[:, :half_spec]
    imag_part = received[:, half_spec:]
    rotated = jnp.concatenate([imag_part, -real_part], axis=1)
    real_vis = contract(received, received)
    imag_vis = contract(rotated, received)
    row_index = jnp.arange(INPUTS, dtype=jnp.int32)[:, None]
    column_index = jnp.arange(INPUTS, dtype=jnp.int32)[None, :]
    packed = jnp.where(column_index <= row_index, real_vis, imag_vis)
    partner_rows = lax.dynamic_slice_in_dim(packed, (1 - parity) * half_rows, half_rows, 0)
    own_rows = lax.dynamic_slice_in_dim(packed, parity * half_rows, half_rows, 0)
    summed = own_rows + swapped(partner_rows, "chan", 0)
    return (summed / SPEC).astype(jnp.bfloat16)


def solution(mesh):
    return jax.shard_map(
        on_device,
        mesh=mesh,
        in_specs=(P(("groups", "chan"), None, None), P(("groups", "chan")), P()),
        out_specs=P(("groups", "chan"), None),
        check_vma=False,
    )
```

profile of v0, /device:TPU:0, one launch (start us, length us, event | category | flops | bytes accessed | tf_op | source)
XLA Modules:
  0.0 349.4 jit_solution(1774210906190760884)
XLA Ops:
  0.0 1.9 fusion.17
  1.9 1.0 cosine_convert_fusion
  2.8 40.1 %multiply_convert_fusion = bf16[128,79,2048]{2,0,1:T(8,128)(2,1)} fusion(s32[128,79,2048]{2,0,1:T(8,128)} %param.3, s32[128]{0:T(128)} %param.4), kind=kLoop, calls=%fused_computation | loop fusion | flops 41418752 | bytes 124256768 | tf_op jit(solution)/shard_map/convert_element_type | solution.py:32
  42.9 0.0 copy-start
  43.0 0.0 copy-start.1
  43.0 200.1 %add_convert_fusion.1.clone.5 = bf16[128,64,2048]{2,0,1:T(8,128)(2,1)} fusion(bf16[128,79,2048]{2,0,1:T(8,128)(2,1)} %multiply_convert_fusion, f32[2048]{0:T(1024)S(1)} %bitcast.59, f32[2048]{0:T(1024)S(1)} %bitcast.60, f32[2048]{0:T(1024)S(1)} %bitcast.46, f32[2048]{0:T(1024)S(1)} %bitcast.47, f32[2048]{0:T(1024)S(1)} %bitcast.48, ...), kind=kLoop, calls=%fused_computation.1.clone.clone.clone.clone.2 | loop fusion | flops 805306368 | bytes 570556416 | tf_op jit(solution)/shard_map/reduce_sum | solution.py:55
  243.1 0.0 copy-done
  243.1 0.0 copy-done.1
  243.1 14.6 %multiply_reduce_fusion = (f32[16]{0:T(128)S(1)}, f32[16,128,64]{1,0,2:T(8,128)S(1)}) fusion(bf16[2048,8]{0,1:T(8,128)(2,1)S(1)} %copy-done.1, bf16[2048,8]{0,1:T(8,128)(2,1)S(1)} %copy-done, bf16[128,64,2048]{2,0,1:T(8,128)(2,1)} %add_convert_fusion.1.clone.5), kind=kOutput, calls=%fused_computation.7 | convolution fusion | flops 537264128 | bytes 34144320 | tf_op jit(solution)/shard_map/isn,nk->iks/dot_general | solution.py:52
  257.7 0.1 slice_add_fusion
  257.8 34.9 %psum.7 = f32[8]{0:T(128)S(1)} all-reduce(f32[8]{0:T(128)S(1)} %slice_add_fusion), channel_id=1, replica_groups=mesh['groups'=2,'chan'=16] {'chan'}, use_global_device_ids=true, to_apply=%region_1.2 | all-reduce | flops 8 | bytes 64 | tf_op jit(solution)/shard_map/psum | solution.py:57
  292.7 0.1 pad_maximum_fusion
  292.8 0.1 multiply_convert_fusion.2
  292.9 0.8 copy.5
  293.7 3.7 %all-to-all-start = ((bf16[16,128,64]{1,2,0:T(8,128)(2,1)}), bf16[16,128,64]{1,2,0:T(8,128)(2,1)S(1)}, u32[]{:S(2)}, u32[]{:S(2)}) async-start(bf16[16,128,64]{1,2,0:T(8,128)(2,1)} %bitcast.20), calls=%async_computation | async-start | bytes 524288 | tf_op jit(solution)/shard_map/all_to_all | solution.py:68
  297.4 9.8 %all-to-all-done = bf16[16,128,64]{1,2,0:T(8,128)(2,1)S(1)} async-done(((bf16[16,128,64]{1,2,0:T(8,128)(2,1)}), bf16[16,128,64]{1,2,0:T(8,128)(2,1)S(1)}, u32[]{:S(2)}, u32[]{:S(2)}) %all-to-all-start) | async-done | bytes 262176 | tf_op jit(solution)/shard_map/all_to_all | solution.py:68
  307.3 2.4 fusion.15
  309.7 8.6 %fusion.1 = f32[2048,2048]{1,0:T(8,128)} fusion(f32[2048,2048]{1,0:T(8,128)S(1)} %fusion.15, bf16[2048,32]{0,1:T(8,128)(2,1)S(1)} %get-tuple-element.6, bf16[2048,32]{0,1:T(8,128)(2,1)S(1)} %get-tuple-element.5, bf16[16,128,64]{1,2,0:T(8,128)(2,1)S(1)} %all-to-all-done), kind=kOutput, calls=%fused_computation.4 | convolution fusion | flops 545783808 | bytes 34078720 | tf_op jit(solution)/shard_map/dot_general | solution.py:42
  318.3 7.7 %constant_dynamic-slice_fusion = f32[1024,2048]{1,0:T(8,128)} fusion(f32[2048,2048]{1,0:T(8,128)} %fusion.1, s32[]{:T(128)S(6)} %select_n.29), kind=kLoop, calls=%fused_computation.30 | loop fusion | bytes 16777220 | tf_op jit(solution)/shard_map/dynamic_slice | solution.py:77
  326.0 0.0 collective-permute-start
  326.0 13.5 %collective-permute-done = f32[1024,2048]{1,0:T(8,128)} collective-permute-done((f32[1024,2048]{1,0:T(8,128)}, f32[1024,2048]{1,0:T(8,128)}, u32[]{:S(2)}, u32[]{:S(2)}) %collective-permute-start) | collective-permute-done | bytes 8388640 | tf_op jit(solution)/shard_map/ppermute | solution.py:16
  339.5 10.0 %multiply_convert_fusion.1 = bf16[1024,2048]{1,0:T(8,128)(2,1)} fusion(f32[1024,2048]{1,0:T(8,128)} %collective-permute-done, f32[2048,2048]{1,0:T(8,128)} %fusion.1, s32[]{:T(128)S(6)} %select_n.28), kind=kLoop, calls=%fused_computation.5 | loop fusion | flops 6291456 | bytes 20971524 | tf_op jit(solution)/shard_map/convert_element_type | solution.py:80
  (4 shorter events, 0.1 us)
Async XLA Ops:
  42.9 200.1 %copy-start = (bf16[2048,8]{0,1:T(8,128)(2,1)S(1)}, bf16[2048,8]{0,1:T(8,128)(2,1)}, u32[]{:S(2)}) copy-start(bf16[2048,8]{0,1:T(8,128)(2,1)} %get-tuple-element.23) | copy-start | bytes 98308
  43.0 200.1 %copy-start.1 = (bf16[2048,8]{0,1:T(8,128)(2,1)S(1)}, bf16[2048,8]{0,1:T(8,128)(2,1)}, u32[]{:S(2)}) copy-start(bf16[2048,8]{0,1:T(8,128)(2,1)} %get-tuple-element.24) | copy-start | bytes 98308
  293.7 13.5 %all-to-all-start = ((bf16[16,128,64]{1,2,0:T(8,128)(2,1)}), bf16[16,128,64]{1,2,0:T(8,128)(2,1)S(1)}, u32[]{:S(2)}, u32[]{:S(2)}) async-start(bf16[16,128,64]{1,2,0:T(8,128)(2,1)} %bitcast.20), calls=%async_computation | async-start | bytes 524288 | tf_op jit(solution)/shard_map/all_to_all | solution.py:68
  326.0 13.5 %collective-permute-start = (f32[1024,2048]{1,0:T(8,128)}, f32[1024,2048]{1,0:T(8,128)}, u32[]{:S(2)}, u32[]{:S(2)}) collective-permute-start(f32[1024,2048]{1,0:T(8,128)} %constant_dynamic-slice_fusion), channel_id=1, source_target_pairs={{0,1},{1,0},{2,3},{3,2},{4,5},{5,4},{6,7},{7,6},{8,9},{9,8},{10,11... | collective-permute-start | bytes 25165832 | tf_op jit(solution)/shard_map/ppermute | solution.py:16
where the time goes:
time: 350 us; the launch traced here: 349 us
  other arithmetic  251 us (72%)
  blocking collectives  34.9 us (10%)
  matrix products  25.6 us (7%)
  waiting for transfers between devices  23.3 us (7%)
  local copies, waits for them, and re-layouts  10.4 us (3%)
  starting transfers between devices  3.72 us (1%)
    reduce_sum x1, other arithmetic, on_device(): squares = jnp.sum(spectra * spectra, axis=(0, 2))  200 us
    convert_element_type x1, other arithmetic, polyphase(): samples = (voltages * input_mask[:, None, None]).astype(jnp.bfloat16)  40.1 us
    psum x1, blocking collectives, on_device(): band_total = lax.psum(band_partial, 'chan')  34.9 us
    dot_general x1, matrix products, on_device(): jnp.einsum('isn,nk->iks', filtered, dft_matrix(NFFT, channels), preferred...  14.6 us
    ppermute x1, waiting for transfers between devices, swapped(): lax.ppermute(value, axis, [(i, i ^ 1 << stride) for i in range(lax.axis_s...  13.5 us
    dot_general x2, matrix products, contract(): lax.dot_general(left, right, (((1,), (1,)), ((), ())), preferred_element_...  10.9 us
    convert_element_type x1, other arithmetic, on_device(): return (summed / SPEC).astype(jnp.bfloat16)  9.98 us
    all_to_all x1, waiting for transfers between devices, on_device(): lax.all_to_all(outgoing, 'chan', split_axis=0, concat_axis=1, tiled=True)[0]  9.81 us
  transfers between devices with their start and end apart: 2, of which 2 were waited for; matrix products, arithmetic and copies ran while one was open for 0% of the time, Pallas kernels for 0%

commit v1 on v0

--- a/solution.py
+++ b/solution.py
@@ -10,6 +10,35 @@
 TAPS = 16
 SPEC = 64
 epsilon = 1e-05
+
+
+def list_the_counts(w_in, which_dim, xs):
+    r2 = w_in.shape
+    fresh = w_in.reshape(*r2[:which_dim], xs, r2[which_dim] // xs, *r2[which_dim + 1 :])
+    return jnp.moveaxis(fresh, which_dim, 0)
+
+
+def _plan_halves(xx, row_dim):
+    piece_next = list(xx.shape[1:])
+    piece_next[row_dim] *= xx.shape[0]
+    return jnp.moveaxis(xx, 0, row_dim).reshape(piece_next)
+
+
+def choose_domain(load, mesh_ax, base_x, payload):
+    right_arr = lax.axis_size(mesh_ax)
+    part_next = lax.axis_index(mesh_ax)
+    clean, met_up = (right_arr, part_next)
+    frame_out = list_the_counts(load, base_x, clean)
+    chunks = [frame_out[met_up]]
+    for idx in range(1, clean):
+        mid_arr = frame_out[(met_up + idx) % clean]
+        chunks.append(
+            lax.ppermute(
+                mid_arr, axis_name=mesh_ax, perm=[(t, (t + idx) % clean) for t in range(clean)]
+            )
+        )
+    frame_out = jnp.stack(chunks)[(met_up - jnp.arange(clean)) % clean]
+    return _plan_halves(frame_out, payload)
 
 
 def swapped(value, axis, stride):
@@ -65,7 +94,7 @@
     half_spec = SPEC // 2
     outgoing = by_channel.reshape(local_inputs, 2, channels, 2, half_spec)
     outgoing = outgoing.transpose(2, 3, 0, 1, 4).reshape(devices, local_inputs, SPEC)
-    received = lax.all_to_all(outgoing, "chan", split_axis=0, concat_axis=1, tiled=True)[0]
+    received = choose_domain(outgoing, mesh_ax="chan", base_x=0, payload=1)[0]
     real_part = received[:, :half_spec]
     imag_part = received[:, half_spec:]
     rotated = jnp.concatenate([imag_part, -real_part], axis=1)

time: 350 us -> 359 us (1.026)
  starting transfers between devices: 3.72 us -> 16.5 us
  waiting for transfers between devices: 23.3 us -> 19.5 us
    ppermute x0 -> x15, starting transfers between devices: none -> 14.9 us  [choose_domain(): lax.ppermute(mid_arr, axis_name=mesh_ax, perm=[(t, (t + idx) % clean) for...]
    all_to_all x1 -> x0, waiting for transfers between devices: 9.81 us -> none  [on_device(): lax.all_to_all(outgoing, 'chan', split_axis=0, concat_axis=1, tiled=True)[0]]
    ppermute x0 -> x15, waiting for transfers between devices: none -> 6.34 us  [choose_domain(): lax.ppermute(mid_arr, axis_name=mesh_ax, perm=[(t, (t + idx) % clean) for...]
    all_to_all x1 -> x0, starting transfers between devices: 3.71 us -> none  [on_device(): lax.all_to_all(outgoing, 'chan', split_axis=0, concat_axis=1, tiled=True)[0]]
  transfers between devices with their start and end apart: 2 -> 16, of which waited for: 2 -> 3; matrix products, arithmetic and copies ran while one was open for 0% -> 0% of each run, Pallas kernels for 0% -> 0%
where the time goes in v1:
time: 359 us
  other arithmetic  252 us (70%)
  blocking collectives  34.9 us (10%)
  matrix products  25.6 us (7%)
  waiting for transfers between devices  19.5 us (5%)
  starting transfers between devices  16.5 us (5%)
  local copies, waits for them, and re-layouts  10.5 us (3%)
    reduce_sum x1, other arithmetic, on_device(): squares = jnp.sum(spectra * spectra, axis=(0, 2))  200 us
    convert_element_type x1, other arithmetic, polyphase(): samples = (voltages * input_mask[:, None, None]).astype(jnp.bfloat16)  40.1 us
    psum x1, blocking collectives, on_device(): band_total = lax.psum(band_partial, 'chan')  34.9 us
    ppermute x15, starting transfers between devices, choose_domain(): lax.ppermute(mid_arr, axis_name=mesh_ax, perm=[(t, (t + idx) % clean) for...  14.9 us
    dot_general x1, matrix products, on_device(): jnp.einsum('isn,nk->iks', filtered, dft_matrix(NFFT, channels), preferred...  14.6 us
    ppermute x1, waiting for transfers between devices, swapped(): lax.ppermute(value, axis, [(i, i ^ 1 << stride) for i in range(lax.axis_s...  13.1 us
    dot_general x2, matrix products, contract(): lax.dot_general(left, right, (((1,), (1,)), ((), ())), preferred_element_...  10.9 us
    convert_element_type x1, other arithmetic, on_device(): return (summed / SPEC).astype(jnp.bfloat16)  9.98 us
  transfers between devices with their start and end apart: 16, of which 3 were waited for; matrix products, arithmetic and copies ran while one was open for 0% of the time, Pallas kernels for 0%

profile of v1, /device:TPU:0, one launch (start us, length us, event | category | flops | bytes accessed | tf_op | source)
XLA Modules:
  0.0 359.0 jit_solution(17937786244189427625)
XLA Ops:
  0.0 1.9 fusion.19
  1.9 1.0 cosine_convert_fusion
  2.8 40.1 %multiply_convert_fusion = bf16[128,79,2048]{2,0,1:T(8,128)(2,1)} fusion(s32[128,79,2048]{2,0,1:T(8,128)} %param.3, s32[128]{0:T(128)} %param.4), kind=kLoop, calls=%fused_computation.1 | loop fusion | flops 41418752 | bytes 124256768 | tf_op jit(solution)/shard_map/convert_element_type | solution.py:61
  42.9 0.0 copy-start
  43.0 0.0 copy-start.1
  43.0 200.3 %add_convert_fusion.1.clone.5 = bf16[128,64,2048]{2,0,1:T(8,128)(2,1)} fusion(bf16[128,79,2048]{2,0,1:T(8,128)(2,1)} %multiply_convert_fusion, f32[2048]{0:T(1024)S(1)} %bitcast.124, f32[2048]{0:T(1024)S(1)} %bitcast.125, f32[2048]{0:T(1024)S(1)} %bitcast.111, f32[2048]{0:T(1024)S(1)} %bitcast.112, f32[2048]{0:T(1024)S(1)} %bitcast.113, ...), kind=kLoop, calls=%fused_computation.2.clone.clone.clone.clone.2 | loop fusion | flops 805306368 | bytes 570556416 | tf_op jit(solution)/shard_map/reduce_sum | solution.py:84
  243.3 0.0 copy-done
  243.3 0.0 copy-done.1
  243.3 14.6 %multiply_reduce_fusion = (f32[16]{0:T(128)S(1)}, f32[16,128,64]{1,0,2:T(8,128)S(1)}) fusion(bf16[2048,8]{0,1:T(8,128)(2,1)S(1)} %copy-done.1, bf16[2048,8]{0,1:T(8,128)(2,1)S(1)} %copy-done, bf16[128,64,2048]{2,0,1:T(8,128)(2,1)} %add_convert_fusion.1.clone.5), kind=kOutput, calls=%fused_computation.8 | convolution fusion | flops 537264128 | bytes 34144320 | tf_op jit(solution)/shard_map/isn,nk->iks/dot_general | solution.py:81
  257.9 0.1 slice_add_fusion
  258.0 34.9 %psum.7 = f32[8]{0:T(128)S(1)} all-reduce(f32[8]{0:T(128)S(1)} %slice_add_fusion), channel_id=1, replica_groups=mesh['groups'=2,'chan'=16] {'chan'}, use_global_device_ids=true, to_apply=%region_1.2 | all-reduce | flops 8 | bytes 64 | tf_op jit(solution)/shard_map/psum | solution.py:86
  292.9 0.1 pad_maximum_fusion
  293.0 0.1 multiply_convert_fusion.2
  293.1 0.1 copy.5
  293.3 0.1 dynamic-slice_bitcast_fusion
  293.4 0.1 collective-permute-start
  293.4 0.1 collective-permute-start.1
  293.5 0.1 collective-permute-start.2
  293.6 0.1 collective-permute-start.3
  293.6 0.8 collective-permute-start.4
  294.5 4.8 %collective-permute-done = bf16[1,128,64]{1,2,0:T(8,128)(2,1)S(1)} collective-permute-done((bf16[1,128,64]{1,2,0:T(8,128)(2,1)S(1)}, bf16[1,128,64]{1,2,0:T(8,128)(2,1)S(1)}, u32[]{:S(2)}, u32[]{:S(2)}) %collective-permute-start) | collective-permute-done | bytes 16416 | tf_op jit(solution)/shard_map/ppermute | solution.py:36
  299.3 1.0 collective-permute-start.5
  300.3 0.0 collective-permute-done.1
  300.3 0.0 collective-permute-start.6
  300.3 0.0 collective-permute-done.2
  300.3 3.2 collective-permute-start.7
  303.6 0.0 collective-permute-done.3
  303.6 0.0 collective-permute-start.8
  303.6 0.0 collective-permute-done.4
  303.6 2.7 collective-permute-start.9
  306.3 0.0 collective-permute-done.5
  306.3 3.2 collective-permute-start.10
  309.6 0.0 collective-permute-done.6
  309.6 0.0 collective-permute-start.11
  309.6 0.0 collective-permute-done.7
  309.6 1.5 collective-permute-start.12
  311.1 0.0 collective-permute-done.8
  311.1 1.4 collective-permute-start.13
  312.5 0.0 collective-permute-done.9
  312.5 0.7 collective-permute-start.14
  313.3 0.0 collective-permute-done.10
  313.3 0.0 collective-permute-done.11
  313.3 0.0 collective-permute-done.12
  313.4 1.5 collective-permute-done.13
  314.8 0.0 collective-permute-done.14
  314.9 0.6 gather_fusion
  315.5 2.4 fusion.17
  317.9 8.6 %fusion.1 = f32[2048,2048]{1,0:T(8,128)} fusion(f32[2048,2048]{1,0:T(8,128)S(1)} %fusion.17, bf16[2048,32]{0,1:T(8,128)(2,1)S(1)} %get-tuple-element.6, bf16[2048,32]{0,1:T(8,128)(2,1)S(1)} %get-tuple-element.5, bf16[16,128,64]{1,2,0:T(8,128)(2,1)S(1)} %gather_fusion), kind=kOutput, calls=%fused_computation.5 | convolution fusion | flops 545783808 | bytes 34078720 | tf_op jit(solution)/shard_map/dot_general | solution.py:71
  326.5 7.7 %constant_dynamic-slice_fusion = f32[1024,2048]{1,0:T(8,128)} fusion(f32[2048,2048]{1,0:T(8,128)} %fusion.1, s32[]{:T(128)S(6)} %select_n.193), kind=kLoop, calls=%fused_computation.59 | loop fusion | bytes 16777220 | tf_op jit(solution)/shard_map/dynamic_slice | solution.py:106
  334.2 1.7 collective-permute-start.15
  335.9 13.1 %collective-permute-done.15 = f32[1024,2048]{1,0:T(8,128)} collective-permute-done((f32[1024,2048]{1,0:T(8,128)}, f32[1024,2048]{1,0:T(8,128)}, u32[]{:S(2)}, u32[]{:S(2)}) %collective-permute-start.15) | collective-permute-done | bytes 8388640 | tf_op jit(solution)/shard_map/ppermute | solution.py:45
  349.0 10.0 %multiply_convert_fusion.1 = bf16[1024,2048]{1,0:T(8,128)(2,1)} fusion(f32[1024,2048]{1,0:T(8,128)} %collective-permute-done.15, f32[2048,2048]{1,0:T(8,128)} %fusion.1, s32[]{:T(128)S(6)} %select_n.192), kind=kLoop, calls=%fused_computation.6 | loop fusion | flops 6291456 | bytes 20971524 | tf_op jit(solution)/shard_map/convert_element_type | solution.py:109
  (21 shorter events, 0.2 us)
Async XLA Ops:
  42.9 200.3 %copy-start = (bf16[2048,8]{0,1:T(8,128)(2,1)S(1)}, bf16[2048,8]{0,1:T(8,128)(2,1)}, u32[]{:S(2)}) copy-start(bf16[2048,8]{0,1:T(8,128)(2,1)} %get-tuple-element.39) | copy-start | bytes 98308
  43.0 200.3 %copy-start.1 = (bf16[2048,8]{0,1:T(8,128)(2,1)S(1)}, bf16[2048,8]{0,1:T(8,128)(2,1)}, u32[]{:S(2)}) copy-start(bf16[2048,8]{0,1:T(8,128)(2,1)} %get-tuple-element.40) | copy-start | bytes 98308
  293.4 5.9 %collective-permute-start = (bf16[1,128,64]{1,2,0:T(8,128)(2,1)S(1)}, bf16[1,128,64]{1,2,0:T(8,128)(2,1)S(1)}, u32[]{:S(2)}, u32[]{:S(2)}) collective-permute-start(bf16[1,128,64]{1,2,0:T(8,128)(2,1)S(1)} %get-tuple-element.21), channel_id=1, source_target_pairs={{0,1},{1,2},{2,3},{3,4},{4,5},{5,6},{6,7},{7,8},{8,9},{9,10},{10,1... | collective-permute-start | bytes 49160 | tf_op jit(solution)/shard_map/ppermute | solution.py:36
  293.4 6.9 %collective-permute-start.1 = (bf16[1,128,64]{1,2,0:T(8,128)(2,1)S(1)}, bf16[1,128,64]{1,2,0:T(8,128)(2,1)S(1)}, u32[]{:S(2)}, u32[]{:S(2)}) collective-permute-start(bf16[1,128,64]{1,2,0:T(8,128)(2,1)S(1)} %get-tuple-element.20), channel_id=1, source_target_pairs={{0,2},{1,3},{2,4},{3,5},{4,6},{5,7},{6,8},{7,9},{8,10},{9,11},{10,... | collective-permute-start | bytes 49160 | tf_op jit(solution)/shard_map/ppermute | solution.py:36
  293.5 6.8 %collective-permute-start.2 = (bf16[1,128,64]{1,2,0:T(8,128)(2,1)S(1)}, bf16[1,128,64]{1,2,0:T(8,128)(2,1)S(1)}, u32[]{:S(2)}, u32[]{:S(2)}) collective-permute-start(bf16[1,128,64]{1,2,0:T(8,128)(2,1)S(1)} %get-tuple-element.19), channel_id=1, source_target_pairs={{0,3},{1,4},{2,5},{3,6},{4,7},{5,8},{6,9},{7,10},{8,11},{9,12},{10... | collective-permute-start | bytes 49160 | tf_op jit(solution)/shard_map/ppermute | solution.py:36
  293.6 10.0 %collective-permute-start.3 = (bf16[1,128,64]{1,2,0:T(8,128)(2,1)S(1)}, bf16[1,128,64]{1,2,0:T(8,128)(2,1)S(1)}, u32[]{:S(2)}, u32[]{:S(2)}) collective-permute-start(bf16[1,128,64]{1,2,0:T(8,128)(2,1)S(1)} %get-tuple-element.18), channel_id=1, source_target_pairs={{0,4},{1,5},{2,6},{3,7},{4,8},{5,9},{6,10},{7,11},{8,12},{9,13},{1... | collective-permute-start | bytes 49160 | tf_op jit(solution)/shard_map/ppermute | solution.py:36
  293.6 10.0 %collective-permute-start.4 = (bf16[1,128,64]{1,2,0:T(8,128)(2,1)S(1)}, bf16[1,128,64]{1,2,0:T(8,128)(2,1)S(1)}, u32[]{:S(2)}, u32[]{:S(2)}) collective-permute-start(bf16[1,128,64]{1,2,0:T(8,128)(2,1)S(1)} %get-tuple-element.17), channel_id=1, source_target_pairs={{0,5},{1,6},{2,7},{3,8},{4,9},{5,10},{6,11},{7,12},{8,13},{9,14},{... | collective-permute-start | bytes 49160 | tf_op jit(solution)/shard_map/ppermute | solution.py:36
  299.3 7.0 %collective-permute-start.5 = (bf16[1,128,64]{1,2,0:T(8,128)(2,1)S(1)}, bf16[1,128,64]{1,2,0:T(8,128)(2,1)S(1)}, u32[]{:S(2)}, u32[]{:S(2)}) collective-permute-start(bf16[1,128,64]{1,2,0:T(8,128)(2,1)S(1)} %get-tuple-element.16), channel_id=1, source_target_pairs={{0,6},{1,7},{2,8},{3,9},{4,10},{5,11},{6,12},{7,13},{8,14},{9,15},... | collective-permute-start | bytes 49160 | tf_op jit(solution)/shard_map/ppermute | solution.py:36
  300.3 9.3 %collective-permute-start.6 = (bf16[1,128,64]{1,2,0:T(8,128)(2,1)S(1)}, bf16[1,128,64]{1,2,0:T(8,128)(2,1)S(1)}, u32[]{:S(2)}, u32[]{:S(2)}) collective-permute-start(bf16[1,128,64]{1,2,0:T(8,128)(2,1)S(1)} %get-tuple-element.15), channel_id=1, source_target_pairs={{0,7},{1,8},{2,9},{3,10},{4,11},{5,12},{6,13},{7,14},{8,15},{9,0},... | collective-permute-start | bytes 49160 | tf_op jit(solution)/shard_map/ppermute | solution.py:36
  300.3 9.3 %collective-permute-start.7 = (bf16[1,128,64]{1,2,0:T(8,128)(2,1)S(1)}, bf16[1,128,64]{1,2,0:T(8,128)(2,1)S(1)}, u32[]{:S(2)}, u32[]{:S(2)}) collective-permute-start(bf16[1,128,64]{1,2,0:T(8,128)(2,1)S(1)} %get-tuple-element.14), channel_id=1, source_target_pairs={{0,8},{1,9},{2,10},{3,11},{4,12},{5,13},{6,14},{7,15},{8,0},{9,1},... | collective-permute-start | bytes 49160 | tf_op jit(solution)/shard_map/ppermute | solution.py:36
  303.6 7.5 %collective-permute-start.8 = (bf16[1,128,64]{1,2,0:T(8,128)(2,1)S(1)}, bf16[1,128,64]{1,2,0:T(8,128)(2,1)S(1)}, u32[]{:S(2)}, u32[]{:S(2)}) collective-permute-start(bf16[1,128,64]{1,2,0:T(8,128)(2,1)S(1)} %get-tuple-element.13), channel_id=1, source_target_pairs={{0,9},{1,10},{2,11},{3,12},{4,13},{5,14},{6,15},{7,0},{8,1},{9,2},... | collective-permute-start | bytes 49160 | tf_op jit(solution)/shard_map/ppermute | solution.py:36
  303.6 8.9 %collective-permute-start.9 = (bf16[1,128,64]{1,2,0:T(8,128)(2,1)S(1)}, bf16[1,128,64]{1,2,0:T(8,128)(2,1)S(1)}, u32[]{:S(2)}, u32[]{:S(2)}) collective-permute-start(bf16[1,128,64]{1,2,0:T(8,128)(2,1)S(1)} %get-tuple-element.12), channel_id=1, source_target_pairs={{0,10},{1,11},{2,12},{3,13},{4,14},{5,15},{6,0},{7,1},{8,2},{9,3},... | collective-permute-start | bytes 49160 | tf_op jit(solution)/shard_map/ppermute | solution.py:36
  306.3 7.0 %collective-permute-start.10 = (bf16[1,128,64]{1,2,0:T(8,128)(2,1)S(1)}, bf16[1,128,64]{1,2,0:T(8,128)(2,1)S(1)}, u32[]{:S(2)}, u32[]{:S(2)}) collective-permute-start(bf16[1,128,64]{1,2,0:T(8,128)(2,1)S(1)} %get-tuple-element.11), channel_id=1, source_target_pairs={{0,11},{1,12},{2,13},{3,14},{4,15},{5,0},{6,1},{7,2},{8,3},{9,4},{... | collective-permute-start | bytes 49160 | tf_op jit(solution)/shard_map/ppermute | solution.py:36
  309.6 3.7 %collective-permute-start.11 = (bf16[1,128,64]{1,2,0:T(8,128)(2,1)S(1)}, bf16[1,128,64]{1,2,0:T(8,128)(2,1)S(1)}, u32[]{:S(2)}, u32[]{:S(2)}) collective-permute-start(bf16[1,128,64]{1,2,0:T(8,128)(2,1)S(1)} %get-tuple-element.10), channel_id=1, source_target_pairs={{0,12},{1,13},{2,14},{3,15},{4,0},{5,1},{6,2},{7,3},{8,4},{9,5},{1... | collective-permute-start | bytes 49160 | tf_op jit(solution)/shard_map/ppermute | solution.py:36
  309.6 3.7 %collective-permute-start.12 = (bf16[1,128,64]{1,2,0:T(8,128)(2,1)S(1)}, bf16[1,128,64]{1,2,0:T(8,128)(2,1)S(1)}, u32[]{:S(2)}, u32[]{:S(2)}) collective-permute-start(bf16[1,128,64]{1,2,0:T(8,128)(2,1)S(1)} %get-tuple-element.9), channel_id=1, source_target_pairs={{0,13},{1,14},{2,15},{3,0},{4,1},{5,2},{6,3},{7,4},{8,5},{9,6},{10... | collective-permute-start | bytes 49160 | tf_op jit(solution)/shard_map/ppermute | solution.py:36
  311.1 3.7 %collective-permute-start.13 = (bf16[1,128,64]{1,2,0:T(8,128)(2,1)S(1)}, bf16[1,128,64]{1,2,0:T(8,128)(2,1)S(1)}, u32[]{:S(2)}, u32[]{:S(2)}) collective-permute-start(bf16[1,128,64]{1,2,0:T(8,128)(2,1)S(1)} %get-tuple-element.8), channel_id=1, source_target_pairs={{0,14},{1,15},{2,0},{3,1},{4,2},{5,3},{6,4},{7,5},{8,6},{9,7},{10,... | collective-permute-start | bytes 49160 | tf_op jit(solution)/shard_map/ppermute | solution.py:36
  312.5 2.3 collective-permute-start.14
  334.2 14.8 %collective-permute-start.15 = (f32[1024,2048]{1,0:T(8,128)}, f32[1024,2048]{1,0:T(8,128)}, u32[]{:S(2)}, u32[]{:S(2)}) collective-permute-start(f32[1024,2048]{1,0:T(8,128)} %constant_dynamic-slice_fusion), channel_id=1, source_target_pairs={{0,1},{1,0},{2,3},{3,2},{4,5},{5,4},{6,7},{7,6},{8,9},{9,8},{10,11... | collective-permute-start | bytes 25165832 | tf_op jit(solution)/shard_map/ppermute | solution.py:45
